TPU v7x, 32 devices: a whole 2x2x4 slice. The times are simulated.
32 devices in a mesh: box: 4 (over z), slab: 8 (over y, x, core).
Axes of the slice: x: 2, y: 2, z: 4, core: 2. Of those that a mesh axis runs over, the one named last changes fastest.
Arguments:
- hidden_field: bfloat16 [4, 8, 64, 128, 128], P('box', None, 'slab'), may hold values from -6 to 6
- cone_grad: float32 [256, 128, 128], P(('box', 'slab')), may hold values from -6 to 6
- conv_weight: bfloat16 [8, 27], replicated, may hold values from -0.4375 to 0.4375
- box_lower: int32 [256], P(('box', 'slab')), may hold values from 0 to 3, as said below
- box_upper: int32 [256], P(('box', 'slab')), may hold values from 0 to 3, as said below
- plane_lower: int32 [256], P(('box', 'slab')), may hold values from 0 to 63, as said below
- plane_upper: int32 [256], P(('box', 'slab')), may hold values from 0 to 63, as said below
- weight_lower: int32 [256], P(('box', 'slab')), may hold values from 0 to 256
- weight_upper: int32 [256], P(('box', 'slab')), may hold values from 0 to 256, as said below
Outputs:
- hidden_grad: bfloat16 [4, 8, 64, 128, 128], P('box', None, 'slab')
- weight_grad: float32 [8, 27], replicated
Inputs may be any that keep to these rules, and one draw needn't show every extreme that they name: With g = l // 64 the group of plane l, box_lower[l] is g or g - 1 (never below 0). box_upper[l] = min(box_lower[l] + 1, 3). Each box b has one offset o_b, and for one box, drawn from the seed, o_b = 32; plane_lower[l] = (l + o_b) mod 64 with b = box_lower[l]. plane_upper[l] = (l + o_b) mod 64 with b = box_upper[l], the same offsets. weight_upper[l] = 256 - weight_lower[l].
All inputs are finite; a program needn't handle non-finite values.
Results may differ from a plain program's by a relative error of at most 0.005.
Values may be sent and summed in bfloat16 or wider, within the bound.
A program may use at most 320 MiB of HBM per device.

v0:
```python
import math
import jax
import jax.numpy as jnp
from jax import lax
from jax.sharding import PartitionSpec as P

WDEN = 256


def passed_along(value, axis, steps):
    count = lax.axis_size(axis)
    first, last = (max(0, -steps), min(count, count - steps))
    return lax.ppermute(value, axis, [(source, source + steps) for source in range(first, last)])


def with_halo(cells, sides, width):
    for axis, dim in sides:
        count = lax.axis_size(axis)
        head = lax.slice_in_dim(cells, 0, width, axis=dim)
        tail = lax.slice_in_dim(cells, cells.shape[dim] - width, cells.shape[dim], axis=dim)
        cells = jnp.concatenate(
            [
                lax.ppermute(tail, axis, [(i, (i + 1) % count) for i in range(count)]),
                cells,
                lax.ppermute(head, axis, [((i + 1) % count, i) for i in range(count)]),
            ],
            axis=dim,
        )
    return cells


def wrap_sides(field):
    field = jnp.concatenate([field[:, -1:], field, field[:, :1]], 1)
    return jnp.concatenate([field[:, :, -1:], field, field[:, :, :1]], 2)


def local(
    hidden_field,
    cone_grad,
    conv_weight,
    box_lower,
    box_upper,
    plane_lower,
    plane_upper,
    weight_lower,
    weight_upper,
):
    group = lax.axis_index("box")
    column = lax.axis_index("slab")
    slab_count = lax.axis_size("slab")
    depth = cone_grad.shape[0]
    total_planes = depth * slab_count
    lower = weight_lower.astype(jnp.float32) / WDEN
    upper = weight_upper.astype(jnp.float32) / WDEN
    own_coef = jnp.where(box_lower == group, lower, 0.0) + jnp.where(box_upper == group, upper, 0.0)
    below_coef = jnp.where(box_lower == group - 1, lower, 0.0)
    above_coef = jnp.where(box_upper == group + 1, upper, 0.0)
    for_below = below_coef[:, None, None] * cone_grad
    for_above = above_coef[:, None, None] * cone_grad
    from_above = passed_along(for_below, "box", -1)
    from_below = passed_along(for_above, "box", 1)
    merged = (own_coef[:, None, None] * cone_grad + from_above + from_below).astype(jnp.bfloat16)
    first_plane = jnp.where(box_lower[0] == group, plane_lower[0], plane_upper[0])
    offset = (first_plane - column * depth) % total_planes
    whole = lax.all_gather(merged, "slab", axis=0, tiled=True)
    wanted = (column * depth + jnp.arange(depth, dtype=jnp.int32) - offset) % total_planes
    field_low = jnp.take(whole, wanted, axis=0)
    padded = with_halo(field_low, (("slab", 0),), 1)
    padded = wrap_sides(padded)[None, None]
    channel_count = hidden_field.shape[1]
    kernel = conv_weight.reshape(channel_count, 1, 3, 3, 3)[:, :, ::-1, ::-1, ::-1]
    numbers = ("NCDHW", "OIDHW", "NCDHW")
    hidden_grad = lax.conv_general_dilated(
        padded,
        kernel,
        (1, 1, 1),
        "VALID",
        dimension_numbers=numbers,
        preferred_element_type=jnp.float32,
    )
    hidden_grad = hidden_grad.astype(jnp.bfloat16).reshape(hidden_field.shape)
    as_kernel = hidden_field.reshape(
        channel_count, 1, depth, hidden_field.shape[3], hidden_field.shape[4]
    )
    partial_value = lax.conv_general_dilated(
        padded,
        as_kernel,
        (1, 1, 1),
        "VALID",
        dimension_numbers=numbers,
        preferred_element_type=jnp.float32,
    )
    partial_value = partial_value[0][:, ::-1, ::-1, ::-1].reshape(channel_count, 27)
    total = lax.psum(partial_value, ("box", "slab"))
    cells = lax.axis_size("box") * total_planes * field_low.shape[1] * field_low.shape[2]
    weight_grad = total * (1.0 / math.sqrt(cells))
    return (hidden_grad, weight_grad)


def solution(mesh):
    in_specs = (
        P("box", None, "slab", None, None),
        P(("box", "slab"), None, None),
        P(),
        P(("box", "slab")),
        P(("box", "slab")),
        P(("box", "slab")),
        P(("box", "slab")),
        P(("box", "slab")),
        P(("box", "slab")),
    )
    out_specs = (P("box", None, "slab", None, None), P())
    return jax.shard_map(local, mesh=mesh, in_specs=in_specs, out_specs=out_specs, check_vma=False)
```

profile of v0, /device:TPU:0, one launch (start us, length us, event | category | flops | bytes accessed | tf_op | source)
XLA Modules:
  0.0 805.5 jit_solution(18228177344446519526)
XLA Ops:
  7.2 0.0 copy-start.16
  7.2 0.0 copy-start.17
  7.2 0.0 copy-start.18
  7.2 0.0 all-gather.2.cloned.1.call-start
  7.2 0.7 fusion.3
  8.0 1.2 broadcast_multiply_fusion.1
  9.1 0.0 copy-start.6
  9.2 1.4 collective-permute-start
  10.6 5.6 collective-permute-start.1
  16.2 10.0 %collective-permute-done = f32[8,128,128]{2,1,0:T(8,128)S(1)} collective-permute-done((f32[8,128,128]{2,1,0:T(8,128)S(1)}, f32[8,128,128]{2,1,0:T(8,128)S(1)}, u32[]{:S(2)}, u32[]{:S(2)}) %collective-permute-start) | collective-permute-done | bytes 524320 | tf_op jit(solution)/shard_map/ppermute | solution.py:13
  26.1 1.2 collective-permute-done.1
  27.3 1.9 add_convert_fusion
  29.2 0.0 all-gather.2.cloned.1.call-update
  29.4 30.2 %all-gather.2.cloned.1.call-done = bf16[64,128,128]{2,1,0:T(8,128)(2,1)} async-done(((bf16[8,128,128]{2,1,0:T(8,128)(2,1)}), bf16[64,128,128]{2,1,0:T(8,128)(2,1)}) %all-gather.2.cloned.1.call-update) | async-done | bytes 2097168 | tf_op jit(solution)/shard_map/all_gather | solution.py:65
  59.6 2.2 gather_fusion
  61.8 0.1 broadcast_select_fusion
  61.9 0.3 collective-permute-start.2
  62.3 2.4 collective-permute-start.3
  64.6 69.5 %copy.41 = bf16[8,1,8,128,128]{0,1,4,3,2:T(2,128)(2,1)} copy(bf16[8,1,8,128,128]{4,3,2,0,1:T(8,128)(2,1)S(1)} %bitcast.34) | data formatting | bytes 4194304 | tf_op jit(solution)/shard_map/reshape | solution.py:82
  134.1 0.1 copy.36
  134.2 0.6 reshape.96
  134.9 0.0 collective-permute-done.2
  134.9 0.0 collective-permute-done.3
  134.9 0.1 pad_maximum_fusion.1
  135.0 0.2 fusion.7
  135.2 0.0 copy-start.4
  135.2 0.0 copy-done
  135.2 0.7 copy-done.2
  135.9 0.1 copy-done.4
  136.0 0.6 fusion.15
  136.6 184.9 %copy.40 = bf16[1,1,10,130,130]{1,0,4,3,2:T(2,128)(2,1)} copy(bf16[1,1,10,130,130]{4,3,2,1,0:T(8,128)(2,1)S(1)} %fusion.15) | data formatting | bytes 676000 | tf_op jit(solution)/shard_map/broadcast_in_dim | solution.py:69
  321.5 0.0 copy-done.12
  321.6 0.0 copy-start.5
  321.6 253.9 %fusion.9 = f32[1,8,3,3,3]{1,0,4,3,2:T(1,128)S(1)} fusion(bf16[1,1,10,130,130]{1,0,4,3,2:T(2,128)(2,1)} %copy.40, bf16[8,1,8,128,128]{0,1,4,3,2:T(2,128)(2,1)} %copy.41), kind=kOutput, calls=%fused_computation.40 | convolution fusion | flops 56623104 | bytes 2436016 | tf_op jit(solution)/shard_map/conv_general_dilated | solution.py:85
  575.5 39.6 %psum.7 = f32[8,27]{0,1:T(8,128)S(1)} all-reduce(f32[8,27]{0,1:T(8,128)S(1)} %reshape.75), channel_id=1, replica_groups=mesh['box'=4,'slab'=8] {'box','slab'}, use_global_device_ids=true, to_apply=%region_0.1 | all-reduce | flops 216 | bytes 1728 | tf_op jit(solution)/shard_map/psum | solution.py:94
  615.2 0.7 copy.43
  615.8 0.0 copy-done.5
  615.9 1.3 fusion.16
  617.1 0.4 copy.47
  617.5 0.1 pad.clone
  617.6 0.3 reshape.78
  618.0 0.4 fusion.2
  618.3 33.7 %copy.37 = bf16[1,10,130,8,19]{3,0,4,2,1:T(2,128)(2,1)} copy(bf16[1,10,130,8,19]{2,4,3,1,0:T(8,128)(2,1)S(1)} %fusion.2) | data formatting | bytes 790400 | tf_op jit(solution)/shard_map/conv_general_dilated | solution.py:73
  652.0 112.6 %fusion.10 = bf16[8,128,8,17,8]{4,2,3,1,0:T(8,128)(2,1)} fusion(bf16[1,10,130,8,19]{3,0,4,2,1:T(2,128)(2,1)} %copy.37, bf16[8,1,3,3,3]{0,1,4,3,2:T(2,128)(2,1)S(1)} %copy-done.13), kind=kOutput, calls=%fused_computation.41 | convolution fusion | flops 60162048 | bytes 2623856 | tf_op jit(solution)/shard_map/conv_general_dilated | solution.py:73
  764.6 30.5 %copy.39 = bf16[8,128,8,17,8]{1,4,3,2,0:T(8,128)(2,1)S(1)} copy(bf16[8,128,8,17,8]{4,2,3,1,0:T(8,128)(2,1)} %fusion.10) | data formatting | bytes 4456448 | tf_op jit(solution)/shard_map/conv_general_dilated | solution.py:73
  795.1 0.5 select_convert_fusion
  795.7 0.1 slice_bitcast_fusion
  795.8 2.9 copy.42
  (37 shorter events, 0.2 us)
Async XLA Ops:
  7.2 22.1 %copy-start.16 = (s32[8]{0:T(128)S(1)}, s32[8]{0:T(128)}, u32[]{:S(2)}) copy-start(s32[8]{0:T(128)} %param.12) | copy-start | bytes 100
  7.2 22.1 %copy-start.17 = (s32[8]{0:T(128)S(1)}, s32[8]{0:T(128)}, u32[]{:S(2)}) copy-start(s32[8]{0:T(128)} %param.14) | copy-start | bytes 100
  7.2 22.1 %copy-start.18 = (s32[8]{0:T(128)S(1)}, s32[8]{0:T(128)}, u32[]{:S(2)}) copy-start(s32[8]{0:T(128)} %param.15) | copy-start | bytes 100
  7.2 52.4 %all-gather.2.cloned.1.call-start = ((), (), s32[]{:S(2)}) async-start(), calls=%async_computation | async-start | bytes 2359296 | tf_op jit(solution)/shard_map/all_gather | solution.py:65
  9.1 55.5 %copy-start.6 = (bf16[1,8,8,128,128]{4,3,2,1,0:T(8,128)(2,1)S(1)}, bf16[1,8,8,128,128]{4,3,2,1,0:T(8,128)(2,1)}, u32[]{:S(2)}) copy-start(bf16[1,8,8,128,128]{4,3,2,1,0:T(8,128)(2,1)} %param.9) | copy-start | bytes 6291460
  9.2 17.0 %collective-permute-start = (f32[8,128,128]{2,1,0:T(8,128)S(1)}, f32[8,128,128]{2,1,0:T(8,128)S(1)}, u32[]{:S(2)}, u32[]{:S(2)}) collective-permute-start(f32[8,128,128]{2,1,0:T(8,128)S(1)} %get-tuple-element.8), channel_id=1, source_target_pairs={{8,0},{16,8},{24,16},{9,1},{17,9},{25,17},{10,2},{18,10},{26,18},{... | collective-permute-start | bytes 1572872 | tf_op jit(solution)/shard_map/ppermute | solution.py:13
  10.6 16.7 %collective-permute-start.1 = (f32[8,128,128]{2,1,0:T(8,128)S(1)}, f32[8,128,128]{2,1,0:T(8,128)S(1)}, u32[]{:S(2)}, u32[]{:S(2)}) collective-permute-start(f32[8,128,128]{2,1,0:T(8,128)S(1)} %get-tuple-element.9), channel_id=1, source_target_pairs={{0,8},{8,16},{16,24},{1,9},{9,17},{17,25},{2,10},{10,18},{18,26},{... | collective-permute-start | bytes 1572872 | tf_op jit(solution)/shard_map/ppermute | solution.py:13
  61.9 73.3 %copy-start = (bf16[8,128,128]{2,1,0:T(8,128)(2,1)}, bf16[8,128,128]{2,1,0:T(8,128)(2,1)S(1)}, u32[]{:S(2)}) copy-start(bf16[8,128,128]{2,1,0:T(8,128)(2,1)S(1)} %broadcast_select_fusion) | copy-start | bytes 786436
  61.9 72.9 %collective-permute-start.2 = (bf16[1,128,128]{2,1,0:T(8,128)(2,1)S(1)}, bf16[1,128,128]{2,1,0:T(8,128)(2,1)S(1)}, u32[]{:S(2)}, u32[]{:S(2)}) collective-permute-start(bf16[1,128,128]{2,1,0:T(8,128)(2,1)S(1)} %get-tuple-element.14), channel_id=1, source_target_pairs={{0,1},{1,2},{2,3},{3,4},{4,5},{5,6},{6,7},{7,0},{8,9},{9,10},{10,1... | collective-permute-start | bytes 98312 | tf_op jit(solution)/shard_map/ppermute | solution.py:23
  62.3 72.6 %collective-permute-start.3 = (bf16[1,128,128]{2,1,0:T(8,128)(2,1)S(1)}, bf16[1,128,128]{2,1,0:T(8,128)(2,1)S(1)}, u32[]{:S(2)}, u32[]{:S(2)}) collective-permute-start(bf16[1,128,128]{2,1,0:T(8,128)(2,1)S(1)} %get-tuple-element.15), channel_id=1, source_target_pairs={{1,0},{2,1},{3,2},{4,3},{5,4},{6,5},{7,6},{0,7},{9,8},{10,9},{11,1... | collective-permute-start | bytes 98312 | tf_op jit(solution)/shard_map/ppermute | solution.py:25
  64.6 69.5 %copy-start.14 = (bf16[8,27]{1,0:T(8,128)(2,1)S(1)}, bf16[8,27]{1,0:T(8,128)(2,1)}, u32[]{:S(2)}) copy-start(bf16[8,27]{1,0:T(8,128)(2,1)} %param.11) | copy-start | bytes 1300
  134.9 1.8 copy-start.7
  134.9 1.8 copy-start.9
  134.9 186.7 %copy-start.11 = (bf16[10,1,128]{2,1,0:T(2,128)(2,1)}, bf16[10,1,128]{2,1,0:T(2,128)(2,1)S(1)}, u32[]{:S(2)}) copy-start(bf16[10,1,128]{2,1,0:T(2,128)(2,1)S(1)} %get-tuple-element.12) | copy-start | bytes 7684
  134.9 186.6 %copy-start.12 = (bf16[10,1,128]{2,1,0:T(2,128)(2,1)}, bf16[10,1,128]{2,1,0:T(2,128)(2,1)S(1)}, u32[]{:S(2)}) copy-start(bf16[10,1,128]{2,1,0:T(2,128)(2,1)S(1)} %get-tuple-element.13) | copy-start | bytes 7684
  135.2 0.7 copy-start.2
  135.2 0.8 copy-start.4
  321.6 294.3 %copy-start.1 = (bf16[8,128,128]{2,1,0:T(8,128)(2,1)S(1)}, bf16[8,128,128]{2,1,0:T(8,128)(2,1)}, u32[]{:S(2)}) copy-start(bf16[8,128,128]{2,1,0:T(8,128)(2,1)} %copy-done) | copy-start | bytes 786436
  321.6 294.3 %copy-start.3 = (bf16[10,130,1]{2,1,0:T(8,128)(2,1)S(1)}, bf16[10,130,1]{2,1,0:T(8,128)(2,1)}, u32[]{:S(2)}) copy-start(bf16[10,130,1]{2,1,0:T(8,128)(2,1)} %copy-done.2) | copy-start | bytes 7804
  321.6 294.3 %copy-start.5 = (bf16[10,130,1]{2,1,0:T(8,128)(2,1)S(1)}, bf16[10,130,1]{2,1,0:T(8,128)(2,1)}, u32[]{:S(2)}) copy-start(bf16[10,130,1]{2,1,0:T(8,128)(2,1)} %copy-done.4) | copy-start | bytes 7804
  321.6 294.3 %copy-start.8 = (bf16[1,128,128]{2,1,0:T(8,128)(2,1)S(1)}, bf16[1,128,128]{2,1,0:T(8,128)(2,1)}, u32[]{:S(2)}) copy-start(bf16[1,128,128]{2,1,0:T(8,128)(2,1)} %copy-done.7) | copy-start | bytes 98308
  321.6 294.3 %copy-start.10 = (bf16[1,128,128]{2,1,0:T(8,128)(2,1)S(1)}, bf16[1,128,128]{2,1,0:T(8,128)(2,1)}, u32[]{:S(2)}) copy-start(bf16[1,128,128]{2,1,0:T(8,128)(2,1)} %copy-done.9) | copy-start | bytes 98308
  618.3 33.7 %copy-start.13 = (bf16[8,1,3,3,3]{0,1,4,3,2:T(2,128)(2,1)S(1)}, bf16[8,1,3,3,3]{0,1,4,3,2:T(2,128)(2,1)}, u32[]{:S(2)}) copy-start(bf16[8,1,3,3,3]{0,1,4,3,2:T(2,128)(2,1)} %reshape.96) | copy-start | bytes 1300
  764.6 30.5 %copy-start.15 = (pred[8,17]{1,0:T(8,128)(4,1)S(1)}, pred[8,17]{1,0:T(8,128)(4,1)}, u32[]{:S(2)}) copy-start(pred[8,17]{1,0:T(8,128)(4,1)} %constant.70) | copy-start | bytes 412
Sparse Core Ops, SparseCore 0:
  29.3 30.2 all-gather.1
where the time goes:
time: 806 us
  matrix products  366 us (45%)
  local copies, waits for them, and re-layouts  327 us (41%)
  waiting for transfers between devices  41.4 us (5%)
  blocking collectives  39.6 us (5%)
  between operations  14.5 us (2%)
  starting transfers between devices  9.75 us (1%)
    conv_general_dilated x1, matrix products, local(): lax.conv_general_dilated(padded, as_kernel, (1, 1, 1), 'VALID', dimension...  254 us
    broadcast_in_dim x2, local copies, waits for them, and re-layouts, local(): padded = wrap_sides(padded)[None, None]  185 us
    conv_general_dilated x1, matrix products, local(): lax.conv_general_dilated(padded, kernel, (1, 1, 1), 'VALID', dimension_nu...  113 us
    reshape x1, local copies, waits for them, and re-layouts, local(): hidden_field.reshape(channel_count, 1, depth, hidden_field.shape[3], hidd...  69.5 us
    conv_general_dilated x4, local copies, waits for them, and re-layouts, local(): lax.conv_general_dilated(padded, kernel, (1, 1, 1), 'VALID', dimension_nu...  64.5 us
    psum x1, blocking collectives, local(): total = lax.psum(partial_value, ('box', 'slab'))  39.6 us
    all_gather x1, waiting for transfers between devices, local(): whole = lax.all_gather(merged, 'slab', axis=0, tiled=True)  30.2 us
  transfers between devices with their start and end apart: 5, of which 3 were waited for; matrix products, arithmetic and copies ran while one was open for 9% of the time, Pallas kernels for 0%

commit v1 on v0

--- a/solution.py
+++ b/solution.py
@@ -3,6 +3,7 @@
 import jax.numpy as jnp
 from jax import lax
 from jax.sharding import PartitionSpec as P
+from jax.lax import axis_index, axis_size, ppermute
 
 WDEN = 256
 
@@ -62,7 +63,23 @@
     merged = (own_coef[:, None, None] * cone_grad + from_above + from_below).astype(jnp.bfloat16)
     first_plane = jnp.where(box_lower[0] == group, plane_lower[0], plane_upper[0])
     offset = (first_plane - column * depth) % total_planes
-    whole = lax.all_gather(merged, "slab", axis=0, tiled=True)
+
+    def expand_trails(shard_in):
+        n_lanes = axis_size("slab")
+        vals = [shard_in]
+        for num in range(1, n_lanes):
+            vals.append(
+                ppermute(
+                    vals[num - 1],
+                    axis_name="slab",
+                    perm=[(p, (p - 1) % n_lanes) for p in range(n_lanes)],
+                )
+            )
+        mat_out = jnp.concatenate(vals, axis=0)
+        a_next = jnp.roll(mat_out, axis_index("slab") * shard_in.shape[0], axis=0)
+        return a_next
+
+    whole = expand_trails(merged)
     wanted = (column * depth + jnp.arange(depth, dtype=jnp.int32) - offset) % total_planes
     field_low = jnp.take(whole, wanted, axis=0)
     padded = with_halo(field_low, (("slab", 0),), 1)

time: 806 us -> 841 us (1.043); the launches traced: 806 us -> 832 us
  local copies, waits for them, and re-layouts: 327 us -> 355 us
  starting transfers between devices: 9.75 us -> 27.4 us
  between operations: 14.5 us -> 2.91 us
  waiting for transfers between devices: 41.4 us -> 32 us
    all_gather x1 -> x0, waiting for transfers between devices: 30.2 us -> none  [local(): whole = lax.all_gather(merged, 'slab', axis=0, tiled=True)]
    ppermute x0 -> x7, waiting for transfers between devices: none -> 20.8 us  [expand_trails(): ppermute(vals[num - 1], axis_name='slab', perm=[(p, (p - 1) % n_lanes) fo...]
    ppermute x0 -> x7, starting transfers between devices: none -> 17.7 us  [expand_trails(): ppermute(vals[num - 1], axis_name='slab', perm=[(p, (p - 1) % n_lanes) fo...]
    reshape x1, local copies, waits for them, and re-layouts: 69.5 us -> 86.2 us  [local(): hidden_field.reshape(channel_count, 1, depth, hidden_field.shape[3], hidd...]
    unnamed x43 -> x49, local copies, waits for them, and re-layouts: 4.93 us -> 15 us
  transfers between devices with their start and end apart: 5 -> 11, of which waited for: 3 -> 9; matrix products, arithmetic and copies ran while one was open for 9% -> 11% of each run, Pallas kernels for 0% -> 0%
where the time goes in v1:
time: 841 us; the launch traced here: 832 us
  matrix products  367 us (44%)
  local copies, waits for them, and re-layouts  355 us (42%)
  blocking collectives  40.9 us (5%)
  waiting for transfers between devices  32 us (4%)
  starting transfers between devices  27.4 us (3%)
    conv_general_dilated x1, matrix products, local(): lax.conv_general_dilated(padded, as_kernel, (1, 1, 1), 'VALID', dimension...  254 us
    broadcast_in_dim x2, local copies, waits for them, and re-layouts, local(): padded = wrap_sides(padded)[None, None]  185 us
    conv_general_dilated x1, matrix products, local(): lax.conv_general_dilated(padded, kernel, (1, 1, 1), 'VALID', dimension_nu...  113 us
    reshape x1, local copies, waits for them, and re-layouts, local(): hidden_field.reshape(channel_count, 1, depth, hidden_field.shape[3], hidd...  86.2 us
    conv_general_dilated x4, local copies, waits for them, and re-layouts, local(): lax.conv_general_dilated(padded, kernel, (1, 1, 1), 'VALID', dimension_nu...  64.7 us
    psum x1, blocking collectives, local(): total = lax.psum(partial_value, ('box', 'slab'))  40.9 us
    ppermute x7, waiting for transfers between devices, expand_trails(): ppermute(vals[num - 1], axis_name='slab', perm=[(p, (p - 1) % n_lanes) fo...  20.8 us
    ppermute x7, starting transfers between devices, expand_trails(): ppermute(vals[num - 1], axis_name='slab', perm=[(p, (p - 1) % n_lanes) fo...  17.7 us
  transfers between devices with their start and end apart: 11, of which 9 were waited for; matrix products, arithmetic and copies ran while one was open for 11% of the time, Pallas kernels for 0%

profile of v1, /device:TPU:0, one launch (start us, length us, event | category | flops | bytes accessed | tf_op | source)
XLA Modules:
  0.0 831.7 jit_solution(82397799062177478)
XLA Ops:
  0.6 0.7 fusion.3
  1.4 1.2 broadcast_multiply_fusion.1
  2.5 1.3 collective-permute-start
  3.8 5.6 collective-permute-start.1
  9.4 10.0 %collective-permute-done = f32[8,128,128]{2,1,0:T(8,128)S(1)} collective-permute-done((f32[8,128,128]{2,1,0:T(8,128)S(1)}, f32[8,128,128]{2,1,0:T(8,128)S(1)}, u32[]{:S(2)}, u32[]{:S(2)}) %collective-permute-start) | collective-permute-done | bytes 524320 | tf_op jit(solution)/shard_map/ppermute | solution.py:14
  19.4 1.2 collective-permute-done.1
  20.6 1.9 constant_dynamic-update-slice_fusion.15
  22.5 0.9 collective-permute-start.2
  23.3 3.9 collective-permute-done.2
  27.2 2.8 collective-permute-start.3
  30.0 3.9 collective-permute-done.3
  33.9 2.8 collective-permute-start.4
  36.7 3.9 collective-permute-done.4
  40.6 2.8 collective-permute-start.5
  45.4 1.9 collective-permute-done.5
  47.3 2.8 collective-permute-start.6
  50.2 3.8 collective-permute-done.6
  54.0 2.8 collective-permute-start.7
  56.8 0.7 constant_dynamic-update-slice_fusion.14
  57.5 0.7 constant_dynamic-update-slice_fusion.13
  58.3 0.7 constant_dynamic-update-slice_fusion.12
  59.0 1.7 collective-permute-done.7
  60.7 2.8 collective-permute-start.8
  63.5 0.7 constant_dynamic-update-slice_fusion.11
  64.2 0.7 constant_dynamic-update-slice_fusion.10
  65.0 0.7 constant_dynamic-update-slice_fusion.9
  65.7 1.7 collective-permute-done.8
  67.4 0.7 constant_dynamic-update-slice_fusion.8
  68.1 0.7 constant_dynamic-update-slice_fusion.7
  68.8 0.7 constant_dynamic-update-slice_fusion.6
  69.6 0.7 constant_dynamic-update-slice_fusion.5
  70.3 0.7 constant_dynamic-update-slice_fusion.4
  71.0 0.7 constant_dynamic-update-slice_fusion.3
  71.7 0.7 constant_dynamic-update-slice_fusion.2
  72.5 0.7 constant_dynamic-update-slice_fusion.1
  73.2 0.7 constant_dynamic-update-slice_fusion
  73.9 1.7 constant_dynamic-slice_fusion
  76.3 2.9 collective-permute-start.10
  79.2 86.2 %copy.31 = bf16[8,1,8,128,128]{0,1,4,3,2:T(2,128)(2,1)} copy(bf16[8,1,8,128,128]{4,3,2,0,1:T(8,128)(2,1)} %bitcast.34) | data formatting | bytes 4194304 | tf_op jit(solution)/shard_map/reshape | solution.py:99
  167.9 185.0 %copy.30 = bf16[1,1,10,130,130]{1,0,4,3,2:T(2,128)(2,1)} copy(bf16[1,1,10,130,130]{4,3,2,1,0:T(8,128)(2,1)S(1)} %fusion.15) | data formatting | bytes 676000 | tf_op jit(solution)/shard_map/broadcast_in_dim | solution.py:86
  352.9 254.1 %fusion.9 = f32[1,8,3,3,3]{1,0,4,3,2:T(1,128)S(1)} fusion(bf16[1,1,10,130,130]{1,0,4,3,2:T(2,128)(2,1)} %copy.30, bf16[8,1,8,128,128]{0,1,4,3,2:T(2,128)(2,1)} %copy.31), kind=kOutput, calls=%fused_computation.57 | convolution fusion | flops 56623104 | bytes 2436016 | tf_op jit(solution)/shard_map/conv_general_dilated | solution.py:102
  607.0 40.9 %psum.7 = f32[8,27]{0,1:T(8,128)S(1)} all-reduce(f32[8,27]{0,1:T(8,128)S(1)} %reshape.75), channel_id=1, replica_groups=mesh['box'=4,'slab'=8] {'box','slab'}, use_global_device_ids=true, to_apply=%region_0.1 | all-reduce | flops 216 | bytes 1728 | tf_op jit(solution)/shard_map/psum | solution.py:111
  647.9 0.7 copy.33
  648.6 1.3 fusion.16
  651.2 33.9 %copy.27 = bf16[1,10,130,8,19]{3,0,4,2,1:T(2,128)(2,1)} copy(bf16[1,10,130,8,19]{2,4,3,1,0:T(8,128)(2,1)S(1)} %fusion.2) | data formatting | bytes 790400 | tf_op jit(solution)/shard_map/conv_general_dilated | solution.py:90
  685.1 112.6 %fusion.10 = bf16[8,128,8,17,8]{4,2,3,1,0:T(8,128)(2,1)} fusion(bf16[1,10,130,8,19]{3,0,4,2,1:T(2,128)(2,1)} %copy.27, bf16[8,1,3,3,3]{0,1,4,3,2:T(2,128)(2,1)S(1)} %copy-done.12), kind=kOutput, calls=%fused_computation.58 | convolution fusion | flops 60162048 | bytes 2623856 | tf_op jit(solution)/shard_map/conv_general_dilated | solution.py:90
  797.7 30.5 %copy.29 = bf16[8,128,8,17,8]{1,4,3,2,0:T(8,128)(2,1)S(1)} copy(bf16[8,128,8,17,8]{4,2,3,1,0:T(8,128)(2,1)} %fusion.10) | data formatting | bytes 4456448 | tf_op jit(solution)/shard_map/conv_general_dilated | solution.py:90
  828.9 2.9 copy.32
  (56 shorter events, 5.1 us)
Async XLA Ops:
  2.5 16.8 %collective-permute-start = (f32[8,128,128]{2,1,0:T(8,128)S(1)}, f32[8,128,128]{2,1,0:T(8,128)S(1)}, u32[]{:S(2)}, u32[]{:S(2)}) collective-permute-start(f32[8,128,128]{2,1,0:T(8,128)S(1)} %get-tuple-element.8), channel_id=1, source_target_pairs={{8,0},{16,8},{24,16},{9,1},{17,9},{25,17},{10,2},{18,10},{26,18},{... | collective-permute-start | bytes 1572872 | tf_op jit(solution)/shard_map/ppermute | solution.py:14
  3.8 16.7 %collective-permute-start.1 = (f32[8,128,128]{2,1,0:T(8,128)S(1)}, f32[8,128,128]{2,1,0:T(8,128)S(1)}, u32[]{:S(2)}, u32[]{:S(2)}) collective-permute-start(f32[8,128,128]{2,1,0:T(8,128)S(1)} %get-tuple-element.9), channel_id=1, source_target_pairs={{0,8},{8,16},{16,24},{1,9},{9,17},{17,25},{2,10},{10,18},{18,26},{... | collective-permute-start | bytes 1572872 | tf_op jit(solution)/shard_map/ppermute | solution.py:14
  22.5 4.7 collective-permute-start.2
  27.2 6.7 collective-permute-start.3
  33.9 6.7 collective-permute-start.4
  40.6 6.7 collective-permute-start.5
  47.3 6.7 collective-permute-start.6
  54.0 6.7 collective-permute-start.7
  60.7 6.7 collective-permute-start.8
  76.3 90.2 %copy-start = (bf16[8,128,128]{2,1,0:T(8,128)(2,1)}, bf16[8,128,128]{2,1,0:T(8,128)(2,1)S(1)}, u32[]{:S(2)}) copy-start(bf16[8,128,128]{2,1,0:T(8,128)(2,1)S(1)} %broadcast_select_fusion) | copy-start | bytes 786436
  76.3 89.8 %collective-permute-start.10 = (bf16[1,128,128]{2,1,0:T(8,128)(2,1)S(1)}, bf16[1,128,128]{2,1,0:T(8,128)(2,1)S(1)}, u32[]{:S(2)}, u32[]{:S(2)}) collective-permute-start(bf16[1,128,128]{2,1,0:T(8,128)(2,1)S(1)} %get-tuple-element.15), channel_id=1, source_target_pairs={{1,0},{2,1},{3,2},{4,3},{5,4},{6,5},{7,6},{0,7},{9,8},{10,9},{11,1... | collective-permute-start | bytes 98312 | tf_op jit(solution)/shard_map/ppermute | solution.py:26
  79.2 86.9 %collective-permute-start.9 = (bf16[1,128,128]{2,1,0:T(8,128)(2,1)S(1)}, bf16[1,128,128]{2,1,0:T(8,128)(2,1)S(1)}, u32[]{:S(2)}, u32[]{:S(2)}) collective-permute-start(bf16[1,128,128]{2,1,0:T(8,128)(2,1)S(1)} %get-tuple-element.14), channel_id=1, source_target_pairs={{0,1},{1,2},{2,3},{3,4},{4,5},{5,6},{6,7},{7,0},{8,9},{9,10},{10,1... | collective-permute-start | bytes 98312 | tf_op jit(solution)/shard_map/ppermute | solution.py:24
  79.2 86.2 %copy-start.13 = (bf16[8,27]{1,0:T(8,128)(2,1)S(1)}, bf16[8,27]{1,0:T(8,128)(2,1)}, u32[]{:S(2)}) copy-start(bf16[8,27]{1,0:T(8,128)(2,1)} %param.11) | copy-start | bytes 1300
  166.1 186.8 %copy-start.6 = (bf16[1,128,128]{2,1,0:T(8,128)(2,1)}, bf16[1,128,128]{2,1,0:T(8,128)(2,1)S(1)}, u32[]{:S(2)}) copy-start(bf16[1,128,128]{2,1,0:T(8,128)(2,1)S(1)} %collective-permute-done.10) | copy-start | bytes 98308
  166.1 186.7 %copy-start.7 = (bf16[1,128,128]{2,1,0:T(8,128)(2,1)}, bf16[1,128,128]{2,1,0:T(8,128)(2,1)S(1)}, u32[]{:S(2)}) copy-start(bf16[1,128,128]{2,1,0:T(8,128)(2,1)S(1)} %collective-permute-done.9) | copy-start | bytes 98308
  166.2 0.6 copy-start.8
  166.2 0.6 copy-start.10
  166.5 0.7 copy-start.2
  166.5 0.8 copy-start.4
  352.9 295.7 %copy-start.1 = (bf16[8,128,128]{2,1,0:T(8,128)(2,1)S(1)}, bf16[8,128,128]{2,1,0:T(8,128)(2,1)}, u32[]{:S(2)}) copy-start(bf16[8,128,128]{2,1,0:T(8,128)(2,1)} %copy-done) | copy-start | bytes 786436
  352.9 295.7 %copy-start.3 = (bf16[10,130,1]{2,1,0:T(8,128)(2,1)S(1)}, bf16[10,130,1]{2,1,0:T(8,128)(2,1)}, u32[]{:S(2)}) copy-start(bf16[10,130,1]{2,1,0:T(8,128)(2,1)} %copy-done.2) | copy-start | bytes 7804
  352.9 295.7 %copy-start.5 = (bf16[10,130,1]{2,1,0:T(8,128)(2,1)S(1)}, bf16[10,130,1]{2,1,0:T(8,128)(2,1)}, u32[]{:S(2)}) copy-start(bf16[10,130,1]{2,1,0:T(8,128)(2,1)} %copy-done.4) | copy-start | bytes 7804
  352.9 295.7 %copy-start.9 = (bf16[10,1,128]{2,1,0:T(2,128)(2,1)S(1)}, bf16[10,1,128]{2,1,0:T(2,128)(2,1)}, u32[]{:S(2)}) copy-start(bf16[10,1,128]{2,1,0:T(2,128)(2,1)} %copy-done.8) | copy-start | bytes 7684
  352.9 295.7 %copy-start.11 = (bf16[10,1,128]{2,1,0:T(2,128)(2,1)S(1)}, bf16[10,1,128]{2,1,0:T(2,128)(2,1)}, u32[]{:S(2)}) copy-start(bf16[10,1,128]{2,1,0:T(2,128)(2,1)} %copy-done.10) | copy-start | bytes 7684
  651.2 33.9 %copy-start.12 = (bf16[8,1,3,3,3]{0,1,4,3,2:T(2,128)(2,1)S(1)}, bf16[8,1,3,3,3]{0,1,4,3,2:T(2,128)(2,1)}, u32[]{:S(2)}) copy-start(bf16[8,1,3,3,3]{0,1,4,3,2:T(2,128)(2,1)} %reshape.96) | copy-start | bytes 1300
  797.7 30.5 %copy-start.14 = (pred[8,17]{1,0:T(8,128)(4,1)S(1)}, pred[8,17]{1,0:T(8,128)(4,1)}, u32[]{:S(2)}) copy-start(pred[8,17]{1,0:T(8,128)(4,1)} %constant.86) | copy-start | bytes 412
